TPU v7x, 32 devices: a whole 2x2x4 slice. The times are simulated.
32 devices in a mesh: tile: 8 (over z, y), member: 4 (over x, core).
Axes of the slice: x: 2, y: 2, z: 4, core: 2. Of those that a mesh axis runs over, the one named last changes fastest.
Arguments:
- latent: float32 [4, 4, 64, 8192], P('member', None, None, 'tile'), may hold values from -6 to 6
- noise: float32 [4, 4, 64, 8192], P('member', None, None, 'tile'), may hold values from -6 to 6
- features: bfloat16 [64, 64, 8192], P('member', None, 'tile'), may hold values from -6 to 6
- slot_window: int32 [48], P('tile'), may hold values from -1 to 254, as said below
- timestep: int32 [1], replicated, may hold values from 200 to 999
- time_weight: bfloat16 [64, 64], replicated, may hold values from -0.75 to 0.75
- in_weight: bfloat16 [64, 36], replicated, may hold values from -1 to 1
- conv1_weight: bfloat16 [64, 576], replicated, may hold values from -0.25 to 0.25
- conv2_weight: bfloat16 [64, 576], replicated, may hold values from -0.25 to 0.25
- out_weight: bfloat16 [4, 576], replicated, may hold values from -0.25 to 0.25
- norm1_gain: float32 [64], replicated, may hold values from 0.1 to 1.9
- norm2_gain: float32 [64], replicated, may hold values from 0.1 to 1.9
- norm3_gain: float32 [64], replicated, may hold values from 0.1 to 1.9
Outputs:
- latent_prev: float32 [4, 4, 64, 8192], P('member', None, None, 'tile')
Inputs may be any that keep to these rules, and one draw needn't show every extreme that they name: `slot_window`: entry j of tile t's 6 slots (index t * 6 + j) is -1 for an empty slot or a window whose columns all lie in tiles t - 1 to t + 1; a window may be listed in several slots, and each listing counts.
All inputs are finite; a program needn't handle non-finite values.
Results may differ from a plain program's by a relative error of at most 0.0003.
Values may be sent and summed in bfloat16 or wider, within the bound.
A program may use at most 128 MiB of HBM per device.

v0:
```python
import math
import jax
import jax.numpy as jnp
from jax import lax
from jax.sharding import PartitionSpec as P

LAT = 4
WIN = 64
REACH = 1
TRAIN_STEPS = 1000
STRIDE = 20
GROUPS = 32
norm_epsilon = 1e-05
eta_noise = 0.5
beta_first = 0.00085
beta_last = 0.012


def with_halo(block, sides, width):
    for axis, dim in sides:
        count = lax.axis_size(axis)
        forward = [(i, i + 1) for i in range(count - 1)]
        backward = [(target, source) for source, target in forward]
        low = lax.ppermute(
            lax.slice_in_dim(block, block.shape[dim] - width, None, axis=dim), axis, forward
        )
        high = lax.ppermute(lax.slice_in_dim(block, 0, width, axis=dim), axis, backward)
        block = jnp.concatenate([low, block, high], axis=dim)
    return block


def from_behind(value, axis, by):
    length = lax.axis_size(axis)
    pairs = [(i, i + by) for i in range(length) if 0 <= i + by < length]
    return lax.ppermute(value, axis, pairs)


def plan_terms(timestep):
    betas_root = jnp.linspace(beta_first**0.5, beta_last**0.5, TRAIN_STEPS, dtype=jnp.float32)
    kept = 1.0 - betas_root * betas_root
    step = jnp.arange(TRAIN_STEPS, dtype=jnp.int32)
    current = jnp.prod(jnp.where(step <= timestep[0], kept, 1.0))
    earlier = jnp.prod(jnp.where(step <= timestep[0] - STRIDE, kept, 1.0))
    sigma_sq = eta_noise * eta_noise * (1.0 - earlier) / (1.0 - current) * (1.0 - current / earlier)
    return (current, earlier, sigma_sq)


def time_embed(timestep, time_weight):
    half_width = time_weight.shape[0] // 2
    freqs_row = jnp.exp(-math.log(10000.0) * jnp.arange(half_width, dtype=jnp.float32) / half_width)
    angles = timestep[0].astype(jnp.float32) * freqs_row
    embedding = jnp.concatenate([jnp.cos(angles), jnp.sin(angles)]).astype(jnp.bfloat16)
    return jax.nn.silu(
        jnp.dot(embedding[None, :], time_weight, preferred_element_type=jnp.float32)[0]
    )


def conv_same(activation, weight, window_side):
    cell_count = activation.shape[-1]
    column = jnp.arange(cell_count, dtype=jnp.int32) % window_side
    padded = jnp.pad(activation, ((0, 0), (window_side + 1, window_side + 1)))
    tap_list = []
    for row_shift in (-1, 0, 1):
        for col_shift in (-1, 0, 1):
            anchor = window_side + 1 + row_shift * window_side + col_shift
            tap_piece = padded[:, anchor : anchor + cell_count]
            if col_shift == -1:
                tap_piece = jnp.where(column >= 1, tap_piece, jnp.zeros_like(tap_piece))
            if col_shift == 1:
                tap_piece = jnp.where(
                    column <= window_side - 2, tap_piece, jnp.zeros_like(tap_piece)
                )
            tap_list.append(tap_piece)
    stacked = jnp.concatenate(tap_list, axis=0)
    return jnp.dot(weight, stacked, preferred_element_type=jnp.float32)


def group_norm(hidden, gain):
    channels, cell_count = hidden.shape
    grouped = hidden.reshape(GROUPS, channels // GROUPS * cell_count)
    center = jnp.mean(grouped, axis=1, keepdims=True)
    deviate = grouped - center
    spread_sq = jnp.mean(deviate * deviate, axis=1, keepdims=True)
    normed = (deviate * lax.rsqrt(spread_sq + norm_epsilon)).reshape(channels, cell_count)
    return normed * gain[:, None]


def denoiser(latent_win, feature_win, time_bias, weight_set):
    in_weight, conv1_weight, conv2_weight, out_weight, gain_one, gain_two, gain_three = weight_set
    hidden = conv_same(latent_win, in_weight, WIN) + feature_win.astype(jnp.float32)
    first_act = jax.nn.silu(group_norm(hidden, gain_one)).astype(jnp.bfloat16)
    middle = conv_same(first_act, conv1_weight, WIN) + time_bias[:, None]
    second_act = jax.nn.silu(group_norm(middle, gain_two)).astype(jnp.bfloat16)
    block_out = hidden + conv_same(second_act, conv2_weight, WIN)
    third_act = jax.nn.silu(group_norm(block_out, gain_three)).astype(jnp.bfloat16)
    return conv_same(third_act, out_weight, WIN)


def denoise_update(state_now, eps_mean, noise_draw, current, earlier, sigma_sq):
    clean_est = (state_now - jnp.sqrt(1.0 - current) * eps_mean) / jnp.sqrt(current)
    return (
        jnp.sqrt(earlier) * clean_est
        + jnp.sqrt(1.0 - earlier - sigma_sq) * eps_mean
        + jnp.sqrt(sigma_sq) * noise_draw
    )


def body(
    latent,
    noise,
    features,
    slot_window,
    timestep,
    time_weight,
    in_weight,
    conv1_weight,
    conv2_weight,
    out_weight,
    norm1_gain,
    norm2_gain,
    norm3_gain,
):
    tile_width = latent.shape[-1]
    half_win = WIN // 2
    rim_width = REACH * tile_width
    ext_width = tile_width + 2 * rim_width
    tile_index = lax.axis_index("tile")
    all_channels = lax.all_gather(features, "member", axis=0, tiled=True)
    driver_ext = with_halo(all_channels, (("tile", 2),), rim_width)
    latent_ext = with_halo(latent[0].astype(jnp.bfloat16), (("tile", 2),), rim_width)
    current, earlier, sigma_sq = plan_terms(timestep)
    time_bias = time_embed(timestep, time_weight)
    weight_set = (
        in_weight,
        conv1_weight,
        conv2_weight,
        out_weight,
        norm1_gain,
        norm2_gain,
        norm3_gain,
    )
    listed = slot_window >= 0
    listed_weight = listed.astype(jnp.float32)
    local_start = jnp.where(
        listed, slot_window * half_win - tile_index * tile_width + rim_width, rim_width
    )
    channels = driver_ext.shape[0]

    def one_slot(start_col):
        latent_win = lax.dynamic_slice_in_dim(latent_ext, start_col, WIN, 2).reshape(LAT, WIN * WIN)
        feature_win = lax.dynamic_slice_in_dim(driver_ext, start_col, WIN, 2).reshape(
            channels, WIN * WIN
        )
        return denoiser(latent_win, feature_win, time_bias, weight_set)

    eps_slots = lax.map(one_slot, local_start)

    def add_slot(running, packed):
        start_col, eps_window, weight_one = packed
        current_slab = lax.dynamic_slice_in_dim(running, start_col, WIN, 2)
        updated = current_slab + weight_one * eps_window.reshape(LAT, WIN, WIN)
        return (lax.dynamic_update_slice_in_dim(running, updated, start_col, 2), None)

    partial_ext, ignored = lax.scan(
        add_slot,
        jnp.zeros((LAT, WIN, ext_width), jnp.float32),
        (local_start, eps_slots, listed_weight),
    )
    ext_cols = jnp.arange(ext_width, dtype=jnp.int32)
    inside = (ext_cols[None, :] >= local_start[:, None]) & (
        ext_cols[None, :] < local_start[:, None] + WIN
    )
    cover_ext = jnp.sum(listed_weight[:, None] * inside.astype(jnp.float32), axis=0)
    eps_total = partial_ext[:, :, rim_width : rim_width + tile_width]
    cover_total = cover_ext[rim_width : rim_width + tile_width]
    distance = 1
    low_col = rim_width + distance * tile_width
    sums_piece = partial_ext[:, :, low_col : low_col + tile_width]
    count_piece = cover_ext[low_col : low_col + tile_width]
    got_sums = from_behind(sums_piece.astype(jnp.bfloat16), "tile", distance).astype(
        sums_piece.dtype
    )
    got_count = from_behind(count_piece.astype(jnp.bfloat16), "tile", distance).astype(
        count_piece.dtype
    )
    eps_total = eps_total + got_sums
    cover_total = cover_total + got_count
    distance = 1
    high_col = rim_width - (distance - 1) * tile_width
    low_col = high_col - tile_width
    sums_piece = partial_ext[:, :, low_col:high_col]
    count_piece = cover_ext[low_col:high_col]
    got_sums = from_behind(sums_piece.astype(jnp.bfloat16), "tile", -distance).astype(
        sums_piece.dtype
    )
    got_count = from_behind(count_piece.astype(jnp.bfloat16), "tile", -distance).astype(
        count_piece.dtype
    )
    eps_total = eps_total + got_sums
    cover_total = cover_total + got_count
    eps_mean = eps_total / jnp.maximum(cover_total, 1.0)[None, None, :]
    return denoise_update(latent[0], eps_mean, noise[0], current, earlier, sigma_sq)[None]


def solution(mesh):
    placed = (
        P("member", None, None, "tile"),
        P("member", None, None, "tile"),
        P("member", None, "tile"),
        P("tile"),
        P(),
        P(),
        P(),
        P(),
        P(),
        P(),
        P(),
        P(),
        P(),
    )
    return jax.shard_map(
        body, mesh=mesh, in_specs=placed, out_specs=P("member", None, None, "tile"), check_vma=False
    )
```

profile of v0, /device:TPU:9, one launch (start us, length us, event | category | flops | bytes accessed | tf_op | source)
XLA Modules:
  0.0 678.4 jit_solution(9812453653305107138)
XLA Ops:
  7.3 61.6 %all-gather.2.cloned.1.call-done = bf16[64,64,1024]{2,1,0:T(8,128)(2,1)} async-done(((bf16[16,64,1024]{2,1,0:T(8,128)(2,1)}), bf16[64,64,1024]{2,1,0:T(8,128)(2,1)}) %all-gather.2.cloned.1.call-update) | async-done | bytes 8388624 | tf_op jit(solution)/shard_map/all_gather | solution.py:128
  68.8 3.1 collective-permute-start.2
  71.9 3.1 collective-permute-start.3
  76.3 2.2 collective-permute-start
  78.5 5.1 collective-permute-start.1
  86.0 368.0 %collective-permute-done = bf16[4,64,1024]{2,1,0:T(8,128)(2,1)S(1)} collective-permute-done((bf16[4,64,1024]{2,1,0:T(8,128)(2,1)S(1)}, bf16[4,64,1024]{2,1,0:T(8,128)(2,1)S(1)}, u32[]{:S(2)}, u32[]{:S(2)}) %collective-permute-start) | collective-permute-done | bytes 524320 | tf_op jit(solution)/shard_map/ppermute | solution.py:24
  454.0 2.5 collective-permute-done.1
  456.6 17.6 %pad_maximum_fusion = bf16[64,64,3072]{2,1,0:T(8,128)(2,1)} fusion(bf16[64,64,1024]{2,1,0:T(8,128)(2,1)} %collective-permute-done.3, bf16[64,64,1024]{2,1,0:T(8,128)(2,1)} %all-gather.2.cloned.1.call-done, bf16[64,64,1024]{2,1,0:T(8,128)(2,1)} %collective-permute-done.2), kind=kLoop, calls=%fused_computation.70 | loop fusion | flops 75497472 | bytes 50331648 | tf_op jit(solution)/shard_map/concatenate | solution.py:28
  474.2 127.3 %while.22 = (s32[]{:T(128)}, f32[6,4,4096]{2,1,0:T(4,128)}, s32[6]{0:T(128)S(1)}, bf16[4,64,3072]{2,1,0:T(8,128)(2,1)S(1)}, bf16[64,36]{0,1:T(8,128)(2,1)S(1)}, ...) while((s32[]{:T(128)}, f32[6,4,4096]{2,1,0:T(4,128)}, ...), condition=%wide.region_15.16_spmd, body=%wide.region_2.15_spmd.sunk | while | flops 663355456 | bytes 75635800 | solution.py:156
  477.5 1.6 dynamic-slice_convert_fusion.2
  493.8 1.4 fusion.67
  498.4 2.0 dynamic-slice_convert_fusion.2
  515.1 1.4 fusion.67
  519.6 2.0 dynamic-slice_convert_fusion.2
  536.4 1.4 fusion.67
  540.9 2.0 dynamic-slice_convert_fusion.2
  562.2 2.0 dynamic-slice_convert_fusion.2
  583.5 2.0 dynamic-slice_convert_fusion.2
  601.9 36.7 %while.23 = (s32[]{:T(128)}, f32[4,64,3072]{2,1,0:T(8,128)S(1)}, s32[6]{0:T(128)S(1)}, f32[6]{0:T(128)S(1)}, f32[6,4,4096]{2,1,0:T(4,128)}, /*index=5*/s32[]{:T(128)}, s32[]{:T(128)}, s32[]{:T(128)}) while((s32[]{:T(128)}, f32[4,64,3072]{2,1,0:T(8,128)S(1)}, s32[6]{0:T(128)S(1)}, f32[6]{0:T(128)S(1)}, f32[6,4,4096]{2,1,0:T(4,128)}, ...), condition=%wide.region_17.18_spmd, body=%wide.region_16.17_spmd.sunk | while | flops 32773 | bytes 589983 | solution.py:164
  605.4 1.5 dynamic-slice_multiply_fusion.2
  611.6 1.5 dynamic-slice_multiply_fusion.2
  617.3 1.5 dynamic-slice_multiply_fusion.2
  623.6 1.5 dynamic-slice_multiply_fusion.2
  630.0 1.5 dynamic-slice_multiply_fusion.2
  636.3 1.5 dynamic-slice_multiply_fusion.2
  639.9 1.9 collective-permute-start.4
  641.8 4.3 collective-permute-start.5
  646.1 1.9 collective-permute-start.6
  648.0 4.2 collective-permute-start.7
  657.1 7.4 %collective-permute-done.6 = bf16[1024]{0:T(1024)(128)(2,1)S(1)} collective-permute-done((bf16[1024]{0:T(1024)(128)(2,1)S(1)}, bf16[1024]{0:T(1024)(128)(2,1)S(1)}, u32[]{:S(2)}, u32[]{:S(2)}) %collective-permute-start.6) | collective-permute-done | bytes 2080 | tf_op jit(solution)/shard_map/ppermute | solution.py:35
  664.5 3.7 collective-permute-done.7
  668.2 3.3 fusion.12
  (555 shorter events, 120.1 us)
Async XLA Ops:
  6.5 79.2 %copy-start = (bf16[64,64]{1,0:T(8,128)(2,1)S(1)}, bf16[64,64]{1,0:T(8,128)(2,1)}, u32[]{:S(2)}) copy-start(bf16[64,64]{1,0:T(8,128)(2,1)} %param.22) | copy-start | bytes 24580
  6.5 62.3 %all-gather.2.cloned.1.call-start = ((), (), s32[]{:S(2)}) async-start(), calls=%async_computation | async-start | bytes 10485760 | tf_op jit(solution)/shard_map/all_gather | solution.py:128
  68.8 387.8 %collective-permute-start.2 = (bf16[64,64,1024]{2,1,0:T(8,128)(2,1)}, bf16[64,64,1024]{2,1,0:T(8,128)(2,1)}, u32[]{:S(2)}, u32[]{:S(2)}) collective-permute-start(bf16[64,64,1024]{2,1,0:T(8,128)(2,1)} %all-gather.2.cloned.1.call-done), channel_id=1, source_target_pairs={{0,4},{4,8},{8,12},{12,16},{16,20},{20,24},{24,28},{1,5},{5,9},{9,... | collective-permute-start | bytes 25165832 | tf_op jit(solution)/shard_map/ppermute | solution.py:24
  71.9 384.7 %collective-permute-start.3 = (bf16[64,64,1024]{2,1,0:T(8,128)(2,1)}, bf16[64,64,1024]{2,1,0:T(8,128)(2,1)}, u32[]{:S(2)}, u32[]{:S(2)}) collective-permute-start(bf16[64,64,1024]{2,1,0:T(8,128)(2,1)} %all-gather.2.cloned.1.call-done), channel_id=1, source_target_pairs={{4,0},{8,4},{12,8},{16,12},{20,16},{24,20},{28,24},{5,1},{9,5},{13... | collective-permute-start | bytes 25165832 | tf_op jit(solution)/shard_map/ppermute | solution.py:27
  76.3 377.6 %collective-permute-start = (bf16[4,64,1024]{2,1,0:T(8,128)(2,1)S(1)}, bf16[4,64,1024]{2,1,0:T(8,128)(2,1)S(1)}, u32[]{:S(2)}, u32[]{:S(2)}) collective-permute-start(bf16[4,64,1024]{2,1,0:T(8,128)(2,1)S(1)} %bitcast_convert_fusion), channel_id=1, source_target_pairs={{0,4},{4,8},{8,12},{12,16},{16,20},{20,24},{24,28},{1,5},{5,9},{9,... | collective-permute-start | bytes 1572872 | tf_op jit(solution)/shard_map/ppermute | solution.py:24
  78.5 377.9 %collective-permute-start.1 = (bf16[4,64,1024]{2,1,0:T(8,128)(2,1)S(1)}, bf16[4,64,1024]{2,1,0:T(8,128)(2,1)S(1)}, u32[]{:S(2)}, u32[]{:S(2)}) collective-permute-start(bf16[4,64,1024]{2,1,0:T(8,128)(2,1)S(1)} %bitcast_convert_fusion), channel_id=1, source_target_pairs={{4,0},{8,4},{12,8},{16,12},{20,16},{24,20},{28,24},{5,1},{9,5},{13... | collective-permute-start | bytes 1572872 | tf_op jit(solution)/shard_map/ppermute | solution.py:27
  456.5 17.7 %copy-start.6 = (bf16[64,36]{0,1:T(8,128)(2,1)S(1)}, bf16[64,36]{0,1:T(8,128)(2,1)}, u32[]{:S(2)}) copy-start(bf16[64,36]{0,1:T(8,128)(2,1)} %param.23) | copy-start | bytes 13828
  456.6 17.7 %copy-start.7 = (bf16[4,576]{1,0:T(4,128)(2,1)S(1)}, bf16[4,576]{1,0:T(4,128)(2,1)}, u32[]{:S(2)}) copy-start(bf16[4,576]{1,0:T(4,128)(2,1)} %param.26) | copy-start | bytes 13828
  456.6 17.7 %copy-start.8 = (f32[64]{0:T(128)S(1)}, f32[64]{0:T(128)}, u32[]{:S(2)}) copy-start(f32[64]{0:T(128)} %param.27) | copy-start | bytes 772
  456.6 17.7 %copy-start.9 = (f32[64]{0:T(128)S(1)}, f32[64]{0:T(128)}, u32[]{:S(2)}) copy-start(f32[64]{0:T(128)} %param.28) | copy-start | bytes 772
  456.6 17.7 %copy-start.10 = (f32[64]{0:T(128)S(1)}, f32[64]{0:T(128)}, u32[]{:S(2)}) copy-start(f32[64]{0:T(128)} %param.29) | copy-start | bytes 772
  474.3 2.7 copy-start.2
  486.9 2.0 copy-start.5
  492.9 2.3 copy-start.3
  495.2 2.7 copy-start.2
  508.2 2.0 copy-start.5
  514.2 2.3 copy-start.3
  516.5 2.7 copy-start.2
  529.5 2.0 copy-start.5
  535.5 2.3 copy-start.3
  537.8 2.7 copy-start.2
  550.8 2.0 copy-start.5
  556.8 2.3 copy-start.3
  559.0 2.7 copy-start.2
  578.1 2.3 copy-start.3
  580.3 2.7 copy-start.2
  599.3 2.3 copy-start.3
  638.6 32.9 %copy-start.1 = (bf16[64,64]{1,0:T(8,128)(2,1)S(1)}, bf16[64,64]{1,0:T(8,128)(2,1)}, u32[]{:S(2)}) copy-start(bf16[64,64]{1,0:T(8,128)(2,1)} %param.22) | copy-start | bytes 24580
  639.9 28.3 %collective-permute-start.4 = (bf16[4,64,1024]{2,1,0:T(8,128)(2,1)}, bf16[4,64,1024]{2,1,0:T(8,128)(2,1)}, u32[]{:S(2)}, u32[]{:S(2)}) collective-permute-start(bf16[4,64,1024]{2,1,0:T(8,128)(2,1)} %get-tuple-element.256), channel_id=1, source_target_pairs={{0,4},{4,8},{8,12},{12,16},{16,20},{20,24},{24,28},{1,5},{5,9},{9,... | collective-permute-start | bytes 1572872 | tf_op jit(solution)/shard_map/ppermute | solution.py:35
  641.8 26.4 %collective-permute-start.5 = (bf16[4,64,1024]{2,1,0:T(8,128)(2,1)}, bf16[4,64,1024]{2,1,0:T(8,128)(2,1)}, u32[]{:S(2)}, u32[]{:S(2)}) collective-permute-start(bf16[4,64,1024]{2,1,0:T(8,128)(2,1)} %get-tuple-element.257), channel_id=1, source_target_pairs={{4,0},{8,4},{12,8},{16,12},{20,16},{24,20},{28,24},{5,1},{9,5},{13... | collective-permute-start | bytes 1572872 | tf_op jit(solution)/shard_map/ppermute | solution.py:35
  646.1 18.4 %collective-permute-start.6 = (bf16[1024]{0:T(1024)(128)(2,1)S(1)}, bf16[1024]{0:T(1024)(128)(2,1)S(1)}, u32[]{:S(2)}, u32[]{:S(2)}) collective-permute-start(bf16[1024]{0:T(1024)(128)(2,1)S(1)} %get-tuple-element.258), channel_id=1, source_target_pairs={{0,4},{4,8},{8,12},{12,16},{16,20},{20,24},{24,28},{1,5},{5,9},{9,... | collective-permute-start | bytes 6152 | tf_op jit(solution)/shard_map/ppermute | solution.py:35
  648.0 20.1 %collective-permute-start.7 = (bf16[1024]{0:T(1024)(128)(2,1)S(1)}, bf16[1024]{0:T(1024)(128)(2,1)S(1)}, u32[]{:S(2)}, u32[]{:S(2)}) collective-permute-start(bf16[1024]{0:T(1024)(128)(2,1)S(1)} %get-tuple-element.259), channel_id=1, source_target_pairs={{4,0},{8,4},{12,8},{16,12},{20,16},{24,20},{28,24},{5,1},{9,5},{13... | collective-permute-start | bytes 6152 | tf_op jit(solution)/shard_map/ppermute | solution.py:35
  (8 other events, 15.9 us)
Sparse Core Ops, SparseCore 0:
  8.9 59.8 all-gather.1
where the time goes:
time: 680 us; the launch traced here: 678 us
  waiting for transfers between devices  444 us (65%)
  other arithmetic  95.8 us (14%)
  local copies, waits for them, and re-layouts  44.6 us (7%)
  starting transfers between devices  25.8 us (4%)
  loops' own time  25.2 us (4%)
  matrix products  24.8 us (4%)
  between operations  18.3 us (3%)
    ppermute x2, waiting for transfers between devices, with_halo(): lax.ppermute(lax.slice_in_dim(block, block.shape[dim] - width, None, axis...  368 us
    all_gather x1, waiting for transfers between devices, body(): all_channels = lax.all_gather(features, 'member', axis=0, tiled=True)  61.6 us
    while x108, other arithmetic  27.5 us
    dot_general x24, matrix products, conv_same(): return jnp.dot(weight, stacked, preferred_element_type=jnp.float32)  24.6 us
    concatenate x2, other arithmetic, with_halo(): block = jnp.concatenate([low, block, high], axis=dim)  17.7 us
  transfers between devices with their start and end apart: 9, of which 5 were waited for; matrix products, arithmetic and copies ran while one was open for 1% of the time, Pallas kernels for 0%

commit v1 on v0

--- a/solution.py
+++ b/solution.py
@@ -14,6 +14,19 @@
 eta_noise = 0.5
 beta_first = 0.00085
 beta_last = 0.012
+
+
+def collect(x, axis, dim):
+    ways = lax.axis_size(axis)
+    up = [(d, (d + 1) % ways) for d in range(ways)]
+    down = [(d, (d - 1) % ways) for d in range(ways)]
+    earlier, later = ([x], [x])
+    for _ in range(ways // 2):
+        earlier.append(lax.ppermute(earlier[-1], axis, up))
+    for _ in range((ways - 1) // 2):
+        later.append(lax.ppermute(later[-1], axis, down))
+    line = jnp.concatenate([*earlier[::-1], *later[1:]], axis=dim)
+    return jnp.roll(line, (lax.axis_index(axis) - ways // 2) * x.shape[dim], axis=dim)
 
 
 def with_halo(block, sides, width):
@@ -125,7 +138,7 @@
     rim_width = REACH * tile_width
     ext_width = tile_width + 2 * rim_width
     tile_index = lax.axis_index("tile")
-    all_channels = lax.all_gather(features, "member", axis=0, tiled=True)
+    all_channels = collect(features, "member", 0)
     driver_ext = with_halo(all_channels, (("tile", 2),), rim_width)
     latent_ext = with_halo(latent[0].astype(jnp.bfloat16), (("tile", 2),), rim_width)
     current, earlier, sigma_sq = plan_terms(timestep)

time: 680 us -> 707 us (1.040)
  local copies, waits for them, and re-layouts: 44.6 us -> 75.2 us
  between operations: 18.3 us -> 4.99 us
  waiting for transfers between devices: 444 us -> 453 us
    ppermute x0 -> x3, waiting for transfers between devices: none -> 68.3 us  [the longest x2 68.3 us: collect(): earlier.append(lax.ppermute(earlier[-1], axis, up))]
    all_gather x1 -> x0, waiting for transfers between devices: 61.6 us -> none  [body(): all_channels = lax.all_gather(features, 'member', axis=0, tiled=True)]
    unnamed x14 -> x27, local copies, waits for them, and re-layouts: 0.04 us -> 19 us
    dynamic_slice x0 -> x1, local copies, waits for them, and re-layouts: none -> 8.48 us  [collect(): jnp.roll(line, (lax.axis_index(axis) - ways // 2) * x.shape[dim], axis=dim)]
  transfers between devices with their start and end apart: 9 -> 11, of which waited for: 5 -> 5; matrix products, arithmetic and copies ran while one was open for 1% -> 1% of each run, Pallas kernels for 0% -> 0%
where the time goes in v1:
time: 707 us; the launch traced here: 706 us
  waiting for transfers between devices  453 us (64%)
  other arithmetic  93.3 us (13%)
  local copies, waits for them, and re-layouts  75.2 us (11%)
  starting transfers between devices  29.1 us (4%)
  loops' own time  25.4 us (4%)
  matrix products  24.7 us (3%)
    ppermute x2, waiting for transfers between devices, with_halo(): lax.ppermute(lax.slice_in_dim(block, block.shape[dim] - width, None, axis...  370 us
    ppermute x2, waiting for transfers between devices, collect(): earlier.append(lax.ppermute(earlier[-1], axis, up))  68.3 us
    while x108, other arithmetic  27.5 us
    dot_general x24, matrix products, conv_same(): return jnp.dot(weight, stacked, preferred_element_type=jnp.float32)  24.5 us
    unnamed x27, local copies, waits for them, and re-layouts  19 us
    concatenate x2, other arithmetic, with_halo(): block = jnp.concatenate([low, block, high], axis=dim)  17.7 us
  transfers between devices with their start and end apart: 11, of which 5 were waited for; matrix products, arithmetic and copies ran while one was open for 1% of the time, Pallas kernels for 0%

profile of v1, /device:TPU:9, one launch (start us, length us, event | category | flops | bytes accessed | tf_op | source)
XLA Modules:
  0.0 705.9 jit_solution(10257742721989275901)
XLA Ops:
  0.0 1.8 collective-permute-start.2
  1.8 23.3 %collective-permute-done.2 = bf16[16,64,1024]{2,1,0:T(8,128)(2,1)} collective-permute-done((bf16[16,64,1024]{2,1,0:T(8,128)(2,1)}, bf16[16,64,1024]{2,1,0:T(8,128)(2,1)}, u32[]{:S(2)}, u32[]{:S(2)}) %collective-permute-start.2) | collective-permute-done | bytes 2097184 | tf_op jit(solution)/shard_map/ppermute | solution.py:25
  25.1 2.5 collective-permute-start.3
  27.6 45.0 %collective-permute-done.3 = bf16[16,64,1024]{2,1,0:T(8,128)(2,1)} collective-permute-done((bf16[16,64,1024]{2,1,0:T(8,128)(2,1)}, bf16[16,64,1024]{2,1,0:T(8,128)(2,1)}, u32[]{:S(2)}, u32[]{:S(2)}) %collective-permute-start.3) | collective-permute-done | bytes 2097184 | tf_op jit(solution)/shard_map/ppermute | solution.py:25
  72.5 3.2 constant_dynamic-update-slice_fusion.10
  75.7 3.1 constant_dynamic-update-slice_fusion.9
  80.4 3.2 constant_dynamic-update-slice_fusion.7
  83.5 3.2 constant_dynamic-update-slice_fusion.6
  86.8 3.1 constant_dynamic-update-slice_fusion.5
  91.5 3.2 constant_dynamic-update-slice_fusion.3
  94.6 8.5 %constant_dynamic-slice_fusion.1 = bf16[64,64,1024]{2,1,0:T(8,128)(2,1)} fusion(bf16[128,64,1024]{2,1,0:T(8,128)(2,1)} %constant_dynamic-update-slice_fusion.3, s32[]{:T(128)S(6)} %select_n.248), kind=kLoop, calls=%fused_computation.116 | loop fusion | bytes 16777220 | tf_op jit(solution)/shard_map/jit(_roll_dynamic)/dynamic_slice | solution.py:29
  103.1 3.1 collective-permute-start.5
  106.3 3.0 collective-permute-start.6
  109.4 2.2 collective-permute-start
  111.6 5.0 collective-permute-start.1
  117.7 370.5 %collective-permute-done = bf16[4,64,1024]{2,1,0:T(8,128)(2,1)S(1)} collective-permute-done((bf16[4,64,1024]{2,1,0:T(8,128)(2,1)S(1)}, bf16[4,64,1024]{2,1,0:T(8,128)(2,1)S(1)}, u32[]{:S(2)}, u32[]{:S(2)}) %collective-permute-start) | collective-permute-done | bytes 524320 | tf_op jit(solution)/shard_map/ppermute | solution.py:37
  488.2 2.5 collective-permute-done.1
  490.9 17.6 %pad_maximum_fusion = bf16[64,64,3072]{2,1,0:T(8,128)(2,1)} fusion(bf16[64,64,1024]{2,1,0:T(8,128)(2,1)} %collective-permute-done.6, bf16[64,64,1024]{2,1,0:T(8,128)(2,1)} %constant_dynamic-slice_fusion.1, bf16[64,64,1024]{2,1,0:T(8,128)(2,1)} %collective-permute-done.5), kind=kLoop, calls=%fused_computation.70 | loop fusion | flops 75497472 | bytes 50331648 | tf_op jit(solution)/shard_map/concatenate | solution.py:41
  508.5 127.5 %while.22 = (s32[]{:T(128)}, f32[6,4,4096]{2,1,0:T(4,128)}, s32[6]{0:T(128)S(1)}, bf16[4,64,3072]{2,1,0:T(8,128)(2,1)S(1)}, bf16[64,36]{0,1:T(8,128)(2,1)S(1)}, ...) while((s32[]{:T(128)}, f32[6,4,4096]{2,1,0:T(4,128)}, ...), condition=%wide.region_15.16_spmd, body=%wide.region_2.15_spmd.sunk | while | flops 663355456 | bytes 75635800 | solution.py:169
  511.9 1.6 dynamic-slice_convert_fusion.2
  532.8 2.0 dynamic-slice_convert_fusion.2
  554.1 2.0 dynamic-slice_convert_fusion.2
  575.4 2.0 dynamic-slice_convert_fusion.2
  596.6 2.0 dynamic-slice_convert_fusion.2
  617.9 2.0 dynamic-slice_convert_fusion.2
  636.4 36.7 %while.23 = (s32[]{:T(128)}, f32[4,64,3072]{2,1,0:T(8,128)S(1)}, s32[6]{0:T(128)S(1)}, f32[6]{0:T(128)S(1)}, f32[6,4,4096]{2,1,0:T(4,128)}, /*index=5*/s32[]{:T(128)}, s32[]{:T(128)}, s32[]{:T(128)}) while((s32[]{:T(128)}, f32[4,64,3072]{2,1,0:T(8,128)S(1)}, s32[6]{0:T(128)S(1)}, f32[6]{0:T(128)S(1)}, f32[6,4,4096]{2,1,0:T(4,128)}, ...), condition=%wide.region_17.18_spmd, body=%wide.region_16.17_spmd.sunk | while | flops 32773 | bytes 589983 | solution.py:177
  674.3 1.9 collective-permute-start.7
  676.2 4.3 collective-permute-start.8
  680.5 1.9 collective-permute-start.10
  682.4 3.4 collective-permute-start.9
  690.6 12.0 %collective-permute-done.10 = bf16[1024]{0:T(1024)(128)(2,1)S(1)} collective-permute-done((bf16[1024]{0:T(1024)(128)(2,1)S(1)}, bf16[1024]{0:T(1024)(128)(2,1)S(1)}, u32[]{:S(2)}, u32[]{:S(2)}) %collective-permute-start.10) | collective-permute-done | bytes 2080 | tf_op jit(solution)/shard_map/ppermute | solution.py:48
  702.6 3.3 fusion.12
  (573 shorter events, 133.3 us)
Async XLA Ops:
  0.0 117.5 %copy-start = (bf16[64,64]{1,0:T(8,128)(2,1)S(1)}, bf16[64,64]{1,0:T(8,128)(2,1)}, u32[]{:S(2)}) copy-start(bf16[64,64]{1,0:T(8,128)(2,1)} %param.22) | copy-start | bytes 24580
  0.0 78.8 %copy-start.2 = (bf16[16,64,1024]{2,1,0:T(8,128)(2,1)S(1)}, bf16[16,64,1024]{2,1,0:T(8,128)(2,1)}, u32[]{:S(2)}) copy-start(bf16[16,64,1024]{2,1,0:T(8,128)(2,1)} %param.19) | copy-start | bytes 6291460
  0.0 25.1 %collective-permute-start.2 = (bf16[16,64,1024]{2,1,0:T(8,128)(2,1)}, bf16[16,64,1024]{2,1,0:T(8,128)(2,1)}, u32[]{:S(2)}, u32[]{:S(2)}) collective-permute-start(bf16[16,64,1024]{2,1,0:T(8,128)(2,1)} %param.19), channel_id=1, source_target_pairs={{0,1},{1,2},{2,3},{3,0},{4,5},{5,6},{6,7},{7,4},{8,9},{9,10},{10,1... | collective-permute-start | bytes 6291464 | tf_op jit(solution)/shard_map/ppermute | solution.py:25
  25.1 47.4 %collective-permute-start.3 = (bf16[16,64,1024]{2,1,0:T(8,128)(2,1)}, bf16[16,64,1024]{2,1,0:T(8,128)(2,1)}, u32[]{:S(2)}, u32[]{:S(2)}) collective-permute-start(bf16[16,64,1024]{2,1,0:T(8,128)(2,1)} %collective-permute-done.2), channel_id=1, source_target_pairs={{0,1},{1,2},{2,3},{3,0},{4,5},{5,6},{6,7},{7,4},{8,9},{9,10},{10,1... | collective-permute-start | bytes 6291464 | tf_op jit(solution)/shard_map/ppermute | solution.py:25
  27.6 52.8 %collective-permute-start.4 = (bf16[16,64,1024]{2,1,0:T(8,128)(2,1)}, bf16[16,64,1024]{2,1,0:T(8,128)(2,1)}, u32[]{:S(2)}, u32[]{:S(2)}) collective-permute-start(bf16[16,64,1024]{2,1,0:T(8,128)(2,1)} %param.19), channel_id=1, source_target_pairs={{0,3},{1,0},{2,1},{3,2},{4,7},{5,4},{6,5},{7,6},{8,11},{9,8},{10,9... | collective-permute-start | bytes 6291464 | tf_op jit(solution)/shard_map/ppermute | solution.py:27
  94.6 14.7 %copy-start.3 = (f32[1,4,64,1024]{3,2,1,0:T(8,128)S(1)}, f32[1,4,64,1024]{3,2,1,0:T(8,128)}, u32[]{:S(2)}) copy-start(f32[1,4,64,1024]{3,2,1,0:T(8,128)} %param.17) | copy-start | bytes 3145732
  94.6 22.0 %copy-start.13 = (s32[6]{0:T(128)S(1)}, s32[6]{0:T(128)}, u32[]{:S(2)}) copy-start(s32[6]{0:T(128)} %param.20) | copy-start | bytes 76
  103.1 387.8 %collective-permute-start.5 = (bf16[64,64,1024]{2,1,0:T(8,128)(2,1)}, bf16[64,64,1024]{2,1,0:T(8,128)(2,1)}, u32[]{:S(2)}, u32[]{:S(2)}) collective-permute-start(bf16[64,64,1024]{2,1,0:T(8,128)(2,1)} %constant_dynamic-slice_fusion.1), channel_id=1, source_target_pairs={{0,4},{4,8},{8,12},{12,16},{16,20},{20,24},{24,28},{1,5},{5,9},{9,... | collective-permute-start | bytes 25165832 | tf_op jit(solution)/shard_map/ppermute | solution.py:37
  106.3 384.6 %collective-permute-start.6 = (bf16[64,64,1024]{2,1,0:T(8,128)(2,1)}, bf16[64,64,1024]{2,1,0:T(8,128)(2,1)}, u32[]{:S(2)}, u32[]{:S(2)}) collective-permute-start(bf16[64,64,1024]{2,1,0:T(8,128)(2,1)} %constant_dynamic-slice_fusion.1), channel_id=1, source_target_pairs={{4,0},{8,4},{12,8},{16,12},{20,16},{24,20},{28,24},{5,1},{9,5},{13... | collective-permute-start | bytes 25165832 | tf_op jit(solution)/shard_map/ppermute | solution.py:40
  109.4 378.8 %collective-permute-start = (bf16[4,64,1024]{2,1,0:T(8,128)(2,1)S(1)}, bf16[4,64,1024]{2,1,0:T(8,128)(2,1)S(1)}, u32[]{:S(2)}, u32[]{:S(2)}) collective-permute-start(bf16[4,64,1024]{2,1,0:T(8,128)(2,1)S(1)} %bitcast_convert_fusion), channel_id=1, source_target_pairs={{0,4},{4,8},{8,12},{12,16},{16,20},{20,24},{24,28},{1,5},{5,9},{9,... | collective-permute-start | bytes 1572872 | tf_op jit(solution)/shard_map/ppermute | solution.py:37
  111.6 379.1 %collective-permute-start.1 = (bf16[4,64,1024]{2,1,0:T(8,128)(2,1)S(1)}, bf16[4,64,1024]{2,1,0:T(8,128)(2,1)S(1)}, u32[]{:S(2)}, u32[]{:S(2)}) collective-permute-start(bf16[4,64,1024]{2,1,0:T(8,128)(2,1)S(1)} %bitcast_convert_fusion), channel_id=1, source_target_pairs={{4,0},{8,4},{12,8},{16,12},{20,16},{24,20},{28,24},{5,1},{9,5},{13... | collective-permute-start | bytes 1572872 | tf_op jit(solution)/shard_map/ppermute | solution.py:40
  490.8 17.7 %copy-start.8 = (bf16[64,36]{0,1:T(8,128)(2,1)S(1)}, bf16[64,36]{0,1:T(8,128)(2,1)}, u32[]{:S(2)}) copy-start(bf16[64,36]{0,1:T(8,128)(2,1)} %param.23) | copy-start | bytes 13828
  490.8 17.7 %copy-start.9 = (bf16[4,576]{1,0:T(4,128)(2,1)S(1)}, bf16[4,576]{1,0:T(4,128)(2,1)}, u32[]{:S(2)}) copy-start(bf16[4,576]{1,0:T(4,128)(2,1)} %param.26) | copy-start | bytes 13828
  490.9 17.7 %copy-start.10 = (f32[64]{0:T(128)S(1)}, f32[64]{0:T(128)}, u32[]{:S(2)}) copy-start(f32[64]{0:T(128)} %param.27) | copy-start | bytes 772
  490.9 17.7 %copy-start.11 = (f32[64]{0:T(128)S(1)}, f32[64]{0:T(128)}, u32[]{:S(2)}) copy-start(f32[64]{0:T(128)} %param.28) | copy-start | bytes 772
  490.9 17.7 %copy-start.12 = (f32[64]{0:T(128)S(1)}, f32[64]{0:T(128)}, u32[]{:S(2)}) copy-start(f32[64]{0:T(128)} %param.29) | copy-start | bytes 772
  508.7 2.7 copy-start.4
  527.4 2.3 copy-start.5
  529.7 2.7 copy-start.4
  548.7 2.3 copy-start.5
  550.9 2.7 copy-start.4
  569.9 2.3 copy-start.5
  572.2 2.7 copy-start.4
  591.2 2.3 copy-start.5
  593.5 2.7 copy-start.4
  612.5 2.3 copy-start.5
  614.7 2.7 copy-start.4
  673.0 32.9 %copy-start.1 = (bf16[64,64]{1,0:T(8,128)(2,1)S(1)}, bf16[64,64]{1,0:T(8,128)(2,1)}, u32[]{:S(2)}) copy-start(bf16[64,64]{1,0:T(8,128)(2,1)} %param.22) | copy-start | bytes 24580
  674.3 28.3 %collective-permute-start.7 = (bf16[4,64,1024]{2,1,0:T(8,128)(2,1)}, bf16[4,64,1024]{2,1,0:T(8,128)(2,1)}, u32[]{:S(2)}, u32[]{:S(2)}) collective-permute-start(bf16[4,64,1024]{2,1,0:T(8,128)(2,1)} %get-tuple-element.256), channel_id=1, source_target_pairs={{0,4},{4,8},{8,12},{12,16},{16,20},{20,24},{24,28},{1,5},{5,9},{9,... | collective-permute-start | bytes 1572872 | tf_op jit(solution)/shard_map/ppermute | solution.py:48
  676.2 26.4 %collective-permute-start.8 = (bf16[4,64,1024]{2,1,0:T(8,128)(2,1)}, bf16[4,64,1024]{2,1,0:T(8,128)(2,1)}, u32[]{:S(2)}, u32[]{:S(2)}) collective-permute-start(bf16[4,64,1024]{2,1,0:T(8,128)(2,1)} %get-tuple-element.257), channel_id=1, source_target_pairs={{4,0},{8,4},{12,8},{16,12},{20,16},{24,20},{28,24},{5,1},{9,5},{13... | collective-permute-start | bytes 1572872 | tf_op jit(solution)/shard_map/ppermute | solution.py:48
  680.5 22.1 %collective-permute-start.10 = (bf16[1024]{0:T(1024)(128)(2,1)S(1)}, bf16[1024]{0:T(1024)(128)(2,1)S(1)}, u32[]{:S(2)}, u32[]{:S(2)}) collective-permute-start(bf16[1024]{0:T(1024)(128)(2,1)S(1)} %get-tuple-element.259), channel_id=1, source_target_pairs={{4,0},{8,4},{12,8},{16,12},{20,16},{24,20},{28,24},{5,1},{9,5},{13... | collective-permute-start | bytes 6152 | tf_op jit(solution)/shard_map/ppermute | solution.py:48
  682.4 20.1 %collective-permute-start.9 = (bf16[1024]{0:T(1024)(128)(2,1)S(1)}, bf16[1024]{0:T(1024)(128)(2,1)S(1)}, u32[]{:S(2)}, u32[]{:S(2)}) collective-permute-start(bf16[1024]{0:T(1024)(128)(2,1)S(1)} %get-tuple-element.258), channel_id=1, source_target_pairs={{0,4},{4,8},{8,12},{12,16},{16,20},{20,24},{24,28},{1,5},{5,9},{9,... | collective-permute-start | bytes 6152 | tf_op jit(solution)/shard_map/ppermute | solution.py:48
  (13 other events, 26.1 us)
